TPU v7x, 128 devices: a whole 4x4x4 slice. The times are simulated.
128 devices in a mesh: zero: 16 (over z, x_hi, core), tp: 8 (over x_lo, y).
Axes of the slice: x: 4 (x_hi: 2, x_lo: 2; x = x_hi * 2 + x_lo), y: 4, z: 4, core: 2. Of those that a mesh axis runs over, the one named last changes fastest.
Arguments:
- hidden_in: bfloat16 [8192, 8192], P('zero', 'tp'), may hold values from -8 to 8
- assignment: int32 [8192], replicated, may hold values from 0 to 15, as said below
- attn_gain: bfloat16 [8192], replicated, may hold values from 0.099609375 to 1.8984375
- w_query: bfloat16 [8192, 4096], P('zero', 'tp'), may hold values from -1 to 1
- w_key: bfloat16 [8192, 1024], P('zero', 'tp'), may hold values from -1 to 1
- w_value_proj: bfloat16 [8192, 1024], P('zero', 'tp'), may hold values from -0.0625 to 0.0625
- w_out: bfloat16 [4096, 8192], P('tp', 'zero'), may hold values from -0.09375 to 0.09375
- value_head: bfloat16 [8192], replicated, may hold values from -0.0625 to 0.0625
Outputs:
- scored_hidden: bfloat16 [8192, 8192], P('zero', 'tp')
- values: float32 [8192], P('zero')
Inputs may be any that keep to these rules, and one draw needn't show every extreme that they name: `assignment`: row r belongs to block r // 512; every scorer is assigned exactly 512 rows in all; the rows of one block assigned to one scorer lie next to each other; every block splits its rows over the scorers by the same multiset of counts, each at most 64, and 64 is reached by every block.
All inputs are finite; a program needn't handle non-finite values.
Results may differ from a plain program's by a relative error of at most 0.012.
Values may be sent and summed in bfloat16 or wider, within the bound.
A program may use at most 128 MiB of HBM per device.

v0:
```python
import jax
import jax.numpy as jnp
from jax import lax
from jax.sharding import PartitionSpec as P

HD = 128


EPSILON = 1e-05
ROPE_BASE = 500000.0


def rotary(projected_rows, offsets, head_dim):
    row_count = projected_rows.shape[0]
    head_count = projected_rows.shape[1] // head_dim
    half_dim = head_dim // 2
    frequency = ROPE_BASE ** (-2.0 * jnp.arange(half_dim, dtype=jnp.float32) / head_dim)
    angles = offsets.astype(jnp.float32)[:, None] * frequency[None, :]
    cosine = jnp.cos(angles)[:, None, :]
    sine_part = jnp.sin(angles)[:, None, :]
    shaped = projected_rows.reshape(row_count, head_count, head_dim)
    first_half = shaped[..., :half_dim]
    second_half = shaped[..., half_dim:]
    turned = jnp.concatenate(
        [
            first_half * cosine - second_half * sine_part,
            second_half * cosine + first_half * sine_part,
        ],
        axis=-1,
    )
    return turned.reshape(row_count, head_count * head_dim)


def attend(query_rot, key_rot, value_rows, source, kv_local, head_dim):
    row_count = query_rot.shape[0]
    query_four = query_rot.reshape(row_count, kv_local, -1, head_dim)
    key_three = key_rot.reshape(row_count, kv_local, head_dim)
    value_three = value_rows.reshape(row_count, kv_local, head_dim)
    scores = jnp.einsum(
        "ikgd,jkd->kgij", query_four, key_three, preferred_element_type=jnp.float32
    ) * (1.0 / jnp.sqrt(jnp.float32(head_dim)))
    index_rows = jnp.arange(row_count, dtype=jnp.int32)
    allowed = (source[:, None] == source[None, :]) & (index_rows[None, :] <= index_rows[:, None])
    scores = jnp.where(allowed, scores, jnp.float32(-1e30))
    highest = jnp.max(scores, axis=-1, keepdims=True)
    weights = jnp.exp(scores - highest)
    probs = (weights / jnp.sum(weights, axis=-1, keepdims=True)).astype(jnp.bfloat16)
    mixed = jnp.einsum("kgij,jkd->ikgd", probs, value_three, preferred_element_type=jnp.float32)
    return mixed.astype(jnp.bfloat16).reshape(row_count, -1)


def shards(hidden_in, assignment, attn_gain, w_query, w_key, w_value_proj, w_out, value_head):
    groups = lax.axis_size("zero")
    row_count = hidden_in.shape[0]
    feature_count = hidden_in.shape[1]
    capacity = 2 * row_count // groups
    own_index = lax.axis_index("zero")
    own_dest = lax.dynamic_slice_in_dim(assignment, own_index * row_count, row_count, 0)
    scorer_ids = jnp.arange(groups, dtype=jnp.int32)
    onehot = (own_dest[:, None] == scorer_ids[None, :]).astype(jnp.int32)
    earlier = jnp.cumsum(onehot, axis=0) - onehot
    bucket_rank = jnp.sum(earlier * onehot, axis=1)
    send_slot = own_dest * capacity + bucket_rank
    outgoing = (
        jnp.zeros((groups * capacity, feature_count), hidden_in.dtype).at[send_slot].set(hidden_in)
    )
    incoming = lax.all_to_all(outgoing, "zero", split_axis=0, concat_axis=0, tiled=True)
    block_dest = assignment.reshape(groups, row_count)
    counts = jnp.sum((block_dest == own_index).astype(jnp.int32), axis=1)
    run_ends = jnp.cumsum(counts)
    run_starts = run_ends - counts
    position = jnp.arange(row_count, dtype=jnp.int32)
    source = jnp.sum((run_ends[None, :] <= position[:, None]).astype(jnp.int32), axis=1)
    start_of = jnp.sum(
        jnp.where(source[:, None] == scorer_ids[None, :], run_starts[None, :], 0), axis=1
    )
    offset = position - start_of
    packed = incoming[source * capacity + offset]
    gathered = lax.all_gather(packed, "tp", axis=1, tiled=True)
    wide = gathered.astype(jnp.float32)
    inv_scale = lax.rsqrt(jnp.mean(wide * wide, axis=1, keepdims=True) + EPSILON)
    normed = (wide * inv_scale * attn_gain.astype(jnp.float32)).astype(jnp.bfloat16)

    def add_rows(weight_piece):
        return jnp.dot(normed, weight_piece, preferred_element_type=jnp.float32)

    query_acc = add_rows(lax.all_gather(w_query, "zero", axis=0, tiled=True))
    key_acc = add_rows(lax.all_gather(w_key, "zero", axis=0, tiled=True))
    value_acc = add_rows(lax.all_gather(w_value_proj, "zero", axis=0, tiled=True))
    query_rot = rotary(query_acc, offset, HD).astype(jnp.bfloat16)
    key_rot = rotary(key_acc, offset, HD).astype(jnp.bfloat16)
    value_rows = value_acc.astype(jnp.bfloat16)
    kv_local = w_key.shape[1] // HD
    attended = attend(query_rot, key_rot, value_rows, source, kv_local, HD)
    head_value = value_head.astype(jnp.float32)
    own_head = lax.dynamic_slice_in_dim(
        head_value, lax.axis_index("tp") * feature_count, feature_count, 0
    )
    partial_out = jnp.dot(
        attended,
        lax.all_gather(w_out, "zero", axis=1, tiled=True),
        preferred_element_type=jnp.float32,
    )
    summed = lax.psum_scatter(
        partial_out.astype(jnp.bfloat16), "tp", scatter_dimension=1, tiled=True
    ).astype(jnp.float32)
    residual = packed.astype(jnp.float32) + summed
    squares, along = lax.psum(
        (jnp.sum(residual * residual, axis=1), jnp.sum(residual * own_head[None, :], axis=1)), "tp"
    )
    values = along * lax.rsqrt(squares / gathered.shape[1] + EPSILON)
    return (residual.astype(jnp.bfloat16), values)


def solution(mesh):
    in_specs = (
        P("zero", "tp"),
        P(),
        P(),
        P("zero", "tp"),
        P("zero", "tp"),
        P("zero", "tp"),
        P("tp", "zero"),
        P(),
    )
    out_specs = (P("zero", "tp"), P("zero"))
    return jax.shard_map(shards, mesh=mesh, in_specs=in_specs, out_specs=out_specs, check_vma=False)
```

profile of v0, /device:TPU:1, one launch (start us, length us, event | category | flops | bytes accessed | tf_op | source)
XLA Modules:
  0.0 519.3 jit_solution(17457197304508659695)
XLA Ops:
  7.2 0.8 dynamic-slice_bitcast_fusion
  8.0 0.8 dynamic_slice.6
  8.8 1.1 reduce-window.14
  10.3 0.8 compare_select_fusion.1
  11.0 4.8 scatter_custom_fusion
  15.9 9.3 %all-to-all-start = ((bf16[16,64,1024]{2,1,0:T(8,128)(2,1)}), bf16[16,64,1024]{2,1,0:T(8,128)(2,1)S(1)}, u32[]{:S(2)}, u32[]{:S(2)}) async-start(bf16[16,64,1024]{2,1,0:T(8,128)(2,1)} %bitcast.74), calls=%async_computation | async-start | bytes 4194304 | tf_op jit(solution)/shard_map/all_to_all | solution.py:67
  25.8 27.8 %all-to-all-done = bf16[16,64,1024]{2,1,0:T(8,128)(2,1)S(1)} async-done(((bf16[16,64,1024]{2,1,0:T(8,128)(2,1)}), bf16[16,64,1024]{2,1,0:T(8,128)(2,1)S(1)}, u32[]{:S(2)}, u32[]{:S(2)}) %all-to-all-start) | async-done | bytes 2097184 | tf_op jit(solution)/shard_map/all_to_all | solution.py:67
  53.6 2.8 gather_fusion
  56.5 0.7 all-gather.11.cloned.1.call-update
  57.2 0.7 all-gather.9.cloned.1.call-update
  58.0 0.5 all-gather.7.cloned.1.call-update
  58.5 0.5 all-gather.13.cloned.1.call-update
  59.6 1.0 multiply_cosine_fusion
  60.5 85.9 %all-gather.15.cloned.1.call-done = bf16[512,8192]{1,0:T(8,128)(2,1)} async-done(((bf16[512,1024]{1,0:T(8,128)(2,1)}), bf16[512,8192]{1,0:T(8,128)(2,1)}) %all-gather.15.cloned.1.call-update) | async-done | bytes 8388624 | tf_op jit(solution)/shard_map/all_gather | solution.py:79
  146.4 5.1 fusion
  151.5 69.8 %all-gather.11.cloned.1.call-done = bf16[8192,512]{1,0:T(8,128)(2,1)} async-done(((bf16[512,512]{1,0:T(8,128)(2,1)}), bf16[8192,512]{1,0:T(8,128)(2,1)}) %all-gather.11.cloned.1.call-update) | async-done | bytes 8388624 | tf_op jit(solution)/shard_map/all_gather | solution.py:87
  221.3 11.3 %fusion.39 = f32[512,512]{0,1:T(8,128)S(1)} fusion(bf16[8192,512]{1,0:T(8,128)(2,1)} %all-gather.11.cloned.1.call-done, bf16[512,8192]{1,0:T(8,128)(2,1)} %all-gather.15.cloned.1.call-done, f32[8192]{0:T(1024)S(1)} %convert_element_type.76, f32[512]{0:T(512)S(1)} %add_rsqrt_fusion), kind=kOutput, calls=%fused_computation.77 | convolution fusion | flops 4311744512 | bytes 17860608 | tf_op jit(solution)/shard_map/dot_general | solution.py:85
  233.4 35.7 %all-gather.9.cloned.1.call-done = bf16[8192,128]{1,0:T(8,128)(2,1)} async-done(((bf16[512,128]{1,0:T(8,128)(2,1)}), bf16[8192,128]{1,0:T(8,128)(2,1)}) %all-gather.9.cloned.1.call-update) | async-done | bytes 2097168 | tf_op jit(solution)/shard_map/all_gather | solution.py:88
  269.1 6.7 %convolution_bitcast_fusion = f32[512,1,128]{0,2,1:T(8,128)S(1)} fusion(bf16[8192,128]{1,0:T(8,128)(2,1)} %all-gather.9.cloned.1.call-done, bf16[512,8192]{1,0:T(8,128)(2,1)} %all-gather.15.cloned.1.call-done, f32[8192]{0:T(1024)S(1)} %convert_element_type.76, f32[512]{0:T(512)S(1)} %add_rsqrt_fusion), kind=kOutput, calls=%fused_computation.21 | convolution fusion | flops 1090519040 | bytes 10782720 | tf_op jit(solution)/shard_map/dot_general | solution.py:85
  275.8 0.6 fusion.31
  276.7 1.2 fusion.4
  277.9 1.9 copy-done
  279.8 0.9 fusion.3
  280.7 37.1 %all-gather.7.cloned.1.call-done = bf16[8192,128]{1,0:T(8,128)(2,1)} async-done(((bf16[512,128]{1,0:T(8,128)(2,1)}), bf16[8192,128]{1,0:T(8,128)(2,1)}) %all-gather.7.cloned.1.call-update) | async-done | bytes 2097168 | tf_op jit(solution)/shard_map/all_gather | solution.py:89
  317.8 9.0 %fusion.9 = bf16[128,4,512]{2,0,1:T(8,128)(2,1)S(1)} fusion(f32[4,512]{1,0:T(4,128)S(1)} %fusion.3, f32[4,512]{1,0:T(4,128)S(1)} %get-tuple-element.15, f32[512,512,4]{1,0,2:T(8,128)} %copy-done, pred[512,512]{0,1:T(8,128)(4,1)S(1)} %fusion.15, bf16[8192,128]{1,0:T(8,128)(2,1)} %all-gather.7.cloned.1.call-done, ...), kind=kOutput, calls=%fused_computation.20 | convolution fusion | flops 1364525056 | bytes 15517696 | tf_op jit(solution)/shard_map/kgij,jkd->ikgd/dot_general | solution.py:48
  326.9 69.2 %all-gather.13.cloned.1.call-done = bf16[512,8192]{1,0:T(8,128)(2,1)} async-done(((bf16[512,512]{1,0:T(8,128)(2,1)}), bf16[512,8192]{1,0:T(8,128)(2,1)}) %all-gather.13.cloned.1.call-update) | async-done | bytes 8388624 | tf_op jit(solution)/shard_map/all_gather | solution.py:101
  396.1 10.1 %convolution_convert_fusion = bf16[512,8192]{1,0:T(8,128)(2,1)} fusion(bf16[512,512]{0,1:T(8,128)(2,1)S(1)} %bitcast.76, bf16[512,8192]{1,0:T(8,128)(2,1)} %all-gather.13.cloned.1.call-done), kind=kOutput, calls=%fused_computation.7 | convolution fusion | flops 4299161600 | bytes 17301504 | tf_op jit(solution)/shard_map/dot_general | solution.py:99
  406.2 0.8 dynamic-slice_convert_fusion
  407.0 89.1 %reduce-scatter.2.cloned.1.call-done = bf16[512,1024]{1,0:T(8,128)(2,1)} async-done(((bf16[512,8192]{1,0:T(8,128)(2,1)}), bf16[512,1024]{1,0:T(8,128)(2,1)}) %reduce-scatter.2.cloned.1.call-update) | async-done | bytes 1048592 | tf_op jit(solution)/shard_map/reduce_scatter | solution.py:104
  496.1 2.7 multiply_reduce_fusion
  498.8 13.0 %all-reduce = (f32[512]{0:T(512)S(1)}, f32[512]{0:T(512)S(1)}) all-reduce(f32[512]{0:T(512)S(1)} %get-tuple-element.3, f32[512]{0:T(512)S(1)} %get-tuple-element.2), channel_id=1, replica_groups=mesh['zero'=16,'tp'=8] {'tp'}, use_global_device_ids=true, to_apply=%region_13.14 | all-reduce | flops 1024 | bytes 8192 | tf_op jit(solution)/shard_map/psum | solution.py:108
  511.9 0.6 rsqrt_multiply_fusion
  (41 shorter events, 2.7 us)
Async XLA Ops:
  7.2 18.0 %copy-start.2 = (s32[8192]{0:T(1024)S(1)}, s32[8192]{0:T(1024)}, u32[]{:S(2)}) copy-start(s32[8192]{0:T(1024)} %param.9) | copy-start | bytes 98308
  15.9 37.8 %all-to-all-start = ((bf16[16,64,1024]{2,1,0:T(8,128)(2,1)}), bf16[16,64,1024]{2,1,0:T(8,128)(2,1)S(1)}, u32[]{:S(2)}, u32[]{:S(2)}) async-start(bf16[16,64,1024]{2,1,0:T(8,128)(2,1)} %bitcast.74), calls=%async_computation | async-start | bytes 4194304 | tf_op jit(solution)/shard_map/all_to_all | solution.py:67
  25.1 121.3 %all-gather.15.cloned.1.call-start = ((), (), s32[]{:S(2)}) async-start(), calls=%async_computation.7 | async-start | bytes 9437184 | tf_op jit(solution)/shard_map/all_gather | solution.py:79
  53.6 5.7 %copy-start.3 = (bf16[8192]{0:T(1024)(128)(2,1)S(1)}, bf16[8192]{0:T(1024)(128)(2,1)}, u32[]{:S(2)}) copy-start(bf16[8192]{0:T(1024)(128)(2,1)} %param.10) | copy-start | bytes 49156
  56.4 164.9 %all-gather.11.cloned.1.call-start = ((), (), s32[]{:S(2)}) async-start(), calls=%async_computation.4 | async-start | bytes 8912896 | tf_op jit(solution)/shard_map/all_gather | solution.py:87
  57.2 211.9 %all-gather.9.cloned.1.call-start = ((), (), s32[]{:S(2)}) async-start(), calls=%async_computation.3 | async-start | bytes 2228224 | tf_op jit(solution)/shard_map/all_gather | solution.py:88
  57.9 259.9 %all-gather.7.cloned.1.call-start = ((), (), s32[]{:S(2)}) async-start(), calls=%async_computation.2 | async-start | bytes 2228224 | tf_op jit(solution)/shard_map/all_gather | solution.py:89
  58.5 337.6 %all-gather.13.cloned.1.call-start = ((), (), s32[]{:S(2)}) async-start(), calls=%async_computation.5 | async-start | bytes 8912896 | tf_op jit(solution)/shard_map/all_gather | solution.py:101
  59.1 437.1 %reduce-scatter.2.cloned.1.call-start = ((), (), s32[]{:S(2)}) async-start(), calls=%async_computation.6 | async-start | bytes 9437184 | tf_op jit(solution)/shard_map/reduce_scatter | solution.py:104
  277.9 1.9 copy-start
  406.2 89.9 %copy-start.1 = (bf16[512,1024]{1,0:T(8,128)(2,1)S(1)}, bf16[512,1024]{1,0:T(8,128)(2,1)}, u32[]{:S(2)}) copy-start(bf16[512,1024]{1,0:T(8,128)(2,1)} %gather_fusion) | copy-start | bytes 3145732
Sparse Core Ops, SparseCore 0:
  56.5 89.8 all-gather.14
  148.9 72.3 all-gather.10
  223.8 45.3 all-gather.8
  271.4 46.3 all-gather.6
  320.0 76.0 all-gather.12
  406.3 89.7 reduce-scatter.1
where the time goes:
time: 523 us; the launch traced here: 519 us
  waiting for transfers between devices  417 us (80%)
  matrix products  38.3 us (7%)
  other arithmetic  14.7 us (3%)
  between operations  14.3 us (3%)
  blocking collectives  13 us (2%)
  local copies, waits for them, and re-layouts  12.2 us (2%)
  starting transfers between devices  9.7 us (2%)
    reduce_scatter x1, waiting for transfers between devices, shards(): lax.psum_scatter(partial_out.astype(jnp.bfloat16), 'tp', scatter_dimensio...  89.1 us
    all_gather x1, waiting for transfers between devices, shards(): gathered = lax.all_gather(packed, 'tp', axis=1, tiled=True)  85.9 us
    all_gather x1, waiting for transfers between devices, shards(): query_acc = add_rows(lax.all_gather(w_query, 'zero', axis=0, tiled=True))  69.8 us
    all_gather x1, waiting for transfers between devices, shards(): lax.all_gather(w_out, 'zero', axis=1, tiled=True)  69.2 us
    all_gather x1, waiting for transfers between devices, shards(): lax.all_gather(w_value_proj, 'zero', axis=0, tiled=True)  37.1 us
    all_gather x1, waiting for transfers between devices, shards(): key_acc = add_rows(lax.all_gather(w_key, 'zero', axis=0, tiled=True))  35.7 us
    all_to_all x1, waiting for transfers between devices, shards(): lax.all_to_all(outgoing, 'zero', split_axis=0, concat_axis=0, tiled=True)  27.8 us
    dot_general x2, matrix products, add_rows(): return jnp.dot(normed, weight_piece, preferred_element_type=jnp.float32)  18 us
  transfers between devices with their start and end apart: 7, of which 7 were waited for; matrix products, arithmetic and copies ran while one was open for 7% of the time, Pallas kernels for 0%

commit v1 on v0

v1 whole, which is shorter than its diff:
```python
import jax
import jax.numpy as jnp
from jax import lax
from jax.experimental import pallas as pl
from jax.experimental.pallas import tpu as pltpu
from jax.sharding import PartitionSpec as P

HD = 128
EPSILON = 1e-05
ROPE_BASE = 500000.0
MESH = pl.DeviceIdType.MESH
ROWS = 512
FEATURES = 1024
QKV = 768
CAP = 64
H_PIECES = 4
W_PIECES = 4
A_PIECES = 2
BF16 = jnp.bfloat16
F32 = jnp.float32


def dot(a, b):
    return jnp.dot(a, b, preferred_element_type=F32)


def layer(
    hid, wq, wk, wv, wo, gain_col, slot_row, target_row, offset_col, cosine, sine, head_row,
    out, val_out,
    hg, wg, wog, att, outgoing, incoming, acc, qkv, res, sums, sums_lane,
    h_send, h_recv, w_send, w_recv, o_send, o_recv, r_send, r_recv, a_send, a_recv,
    x_send, x_recv, v_send, v_recv, local_sem,
):
    zero = lax.axis_index("zero")
    tp = lax.axis_index("tp")
    z = lax.div(zero, 4)
    xh = lax.rem(lax.div(zero, 2), 2)
    core = lax.rem(zero, 2)
    xl = lax.div(tp, 4)
    y = lax.rem(tp, 4)
    spot = lax.div(zero, 2)

    def tp_of(far, dy):
        other = lax.rem(xl + far, 2)
        return other * 4 + lax.rem(y + dy + 4, 4)

    def spot_of(far, dz):
        other = lax.rem(xh + far, 2)
        return lax.rem(z + dz + 4, 4) * 2 + other

    def tp_dev(far, dy):
        return (zero, tp_of(far, dy))

    def zero_dev(far, dz):
        return (spot_of(far, dz) * 2 + core, tp)

    sibling = (spot * 2 + (1 - core), tp)

    barrier = pltpu.get_barrier_semaphore()
    greeted = 0
    for k in range(1, 16):
        pl.semaphore_signal(barrier, inc=1, device_id=(lax.rem(zero + k, 16), tp), device_id_type=MESH)
        greeted += 1
    for k in range(1, 8):
        pl.semaphore_signal(barrier, inc=1, device_id=(zero, lax.rem(tp + k, 8)), device_id_type=MESH)
        greeted += 1
    for k in range(8):
        source = (tp * 2 + core, lax.rem(tp + k, 8))
        if k == 0:
            @pl.when(spot != tp)
            def _():
                pl.semaphore_signal(barrier, inc=1, device_id=source, device_id_type=MESH)
        else:
            pl.semaphore_signal(barrier, inc=1, device_id=source, device_id_type=MESH)

    wg[zero, :, 0:512] = (wq[...].astype(F32) * gain_col[...]).astype(BF16)
    wg[zero, :, 512:640] = (wk[...].astype(F32) * gain_col[...]).astype(BF16)
    wg[zero, :, 640:768] = (wv[...].astype(F32) * gain_col[...]).astype(BF16)

    @pl.when(spot != tp)
    def _():
        pl.semaphore_wait(barrier, greeted + 8)

    @pl.when(spot == tp)
    def _():
        pl.semaphore_wait(barrier, greeted + 7)

    started = []

    def send(src, dst, send_sem, recv_sem, device):
        copy = pltpu.make_async_remote_copy(
            src_ref=src, dst_ref=dst, send_sem=send_sem, recv_sem=recv_sem, device_id=device, device_id_type=MESH
        )
        copy.start()
        started.append(copy)

    def arrived(ref, sem):
        pltpu.make_async_remote_copy(
            src_ref=ref, dst_ref=ref, send_sem=sem, recv_sem=sem, device_id=sibling, device_id_type=MESH
        ).wait_recv()

    class Gather:
        def __init__(self, block, index_of, device_of, pieces, send_sems, recv_sems, across_relay, copy_on):
            self.block, self.index_of, self.device_of, self.pieces = block, index_of, device_of, pieces
            self.send_sems, self.recv_sems = send_sems, recv_sems
            self.across_relay, self.copy_on = across_relay, copy_on
            self.count = 0

        def push(self, index, p, device, src=None):
            dst = self.block(index, p)
            send(dst if src is None else src, dst, self.send_sems.at[self.count], self.recv_sems.at[index, p], device)
            self.count += 1

        def own(self, p, src=None):
            index = self.index_of(0, 0)
            self.push(index, p, self.device_of(1, 0), src)
            self.push(index, p, self.device_of(0, 1), src)
            self.push(index, p, self.device_of(0, -1), src)
            self.on(index, p, src)

        def on(self, index, p, src=None):
            if self.copy_on:
                self.push(index, p, sibling, src)

        def wait(self, index, p):
            arrived(self.block(index, p), self.recv_sems.at[index, p])

        def across(self, p):
            index = self.index_of(1, 0)
            self.wait(index, p)
            self.push(index, p, self.device_of(0, 1))
            self.push(index, p, self.device_of(0, -1))
            self.on(index, p)

        def line(self, far, p):
            below, above = self.index_of(far, -1), self.index_of(far, 1)
            relayed = far == 0 or not self.across_relay
            self.wait(below, p)
            if relayed and p < self.pieces // 2:
                self.push(below, p, self.device_of(0, 1))
            self.on(below, p)
            self.wait(above, p)
            if relayed and p >= self.pieces // 2:
                self.push(above, p, self.device_of(0, -1))
            self.on(above, p)

        def opposite(self, far, p):
            index = self.index_of(far, 2)
            self.wait(index, p)
            if far == 0 and self.across_relay:
                self.push(index, p, self.device_of(1, 0))
            self.on(index, p)

    def copied_on(gather):
        for far in range(2):
            for d in (0, 1, -1, 2):
                for p in range(gather.pieces):
                    index = spot_of(far, d) * 2 + (1 - core)
                    gather.wait(index, p)

    h_rows = ROWS // H_PIECES
    hidden = Gather(
        lambda index, p: hg.at[index, pl.ds(p * h_rows, h_rows)], tp_of, tp_dev, H_PIECES, h_send, h_recv, True, False
    )
    w_rows = ROWS // W_PIECES
    weights = Gather(
        lambda index, p: wg.at[index, pl.ds(p * w_rows, w_rows)],
        lambda far, dz: spot_of(far, dz) * 2 + core, zero_dev, W_PIECES, w_send, w_recv, False, True,
    )
    for p in range(max(H_PIECES, W_PIECES)):
        if p < H_PIECES:
            hidden.own(p, hid.at[pl.ds(p * h_rows, h_rows)])
        if p < W_PIECES:
            weights.own(p)
    hg[tp] = hid[...]

    for k in range(8):
        slot = lax.rem(spot + k, 8)
        rows = pl.ds(pl.multiple_of(slot * 64, 64), 64)
        src, dst = wo.at[rows], wog.at[core, tp, rows]
        copy = pltpu.make_async_remote_copy(
            src_ref=src, dst_ref=dst, send_sem=r_send.at[k], recv_sem=r_recv.at[lax.rem(tp - spot + 8, 8)],
            device_id=(slot * 2 + core, spot), device_id_type=MESH,
        )
        if k == 0:
            @pl.when(spot != tp)
            def _():
                copy.start()

            @pl.when(spot == tp)
            def _():
                pltpu.make_async_copy(src, dst, local_sem).start()
        else:
            copy.start()
            started.append(copy)

    for p in range(W_PIECES):
        if p < H_PIECES:
            hidden.across(p)
        weights.across(p)
        if p < H_PIECES:
            hidden.line(0, p)
        weights.line(0, p)
    for p in range(W_PIECES):
        if p < H_PIECES:
            hidden.opposite(0, p)
        weights.line(1, p)
        weights.opposite(0, p)

    my_rows = pl.ds(pl.multiple_of(spot * 64, 64), 64)
    for k in range(8):
        ref = wog.at[core, lax.rem(tp + k, 8), my_rows]
        if k == 0:
            @pl.when(spot != tp)
            def _():
                arrived(ref, r_recv.at[0])
                pltpu.make_async_remote_copy(
                    src_ref=wo.at[my_rows], dst_ref=ref, send_sem=r_send.at[0], recv_sem=r_recv.at[0],
                    device_id=sibling, device_id_type=MESH,
                ).wait_send()

            @pl.when(spot == tp)
            def _():
                pltpu.make_async_copy(wo.at[my_rows], ref, local_sem).wait()
        else:
            arrived(ref, r_recv.at[k])
    w_out = Gather(
        lambda index, p: wog.at[
            lax.rem(index, 2), pl.ds(p * 4, 4), pl.ds(pl.multiple_of(lax.div(index, 2) * 64, 64), 64)
        ],
        lambda far, dz: spot_of(far, dz) * 2 + core, zero_dev, 2, o_send, o_recv, False, True,
    )
    for p in range(W_PIECES):
        weights.opposite(1, p)
        if p < H_PIECES:
            hidden.line(1, p)
    for p in range(H_PIECES):
        hidden.opposite(1, p)
    for p in range(2):
        w_out.own(p)
    copied_on(weights)
    if STOP == 1:
        for p in range(2):
            w_out.across(p)
            w_out.line(0, p)
        for p in range(2):
            w_out.line(1, p)
            w_out.opposite(0, p)
        for p in range(2):
            w_out.opposite(1, p)
        copied_on(w_out)
        for copy in started:
            copy.wait_send()
        out[...] = hg[0]
        val_out[...] = jnp.zeros_like(val_out)
        return

    acc[...] = jnp.zeros_like(acc)
    sums_lane[...] = jnp.zeros_like(sums_lane)

    def project(k, carry):
        half = pl.ds(pl.multiple_of(lax.rem(k, 2) * 512, 512), 512)
        block = hg[lax.div(k, 2), :, half]
        acc[...] += dot(block, wg[k])
        wide = block.astype(F32)
        squares = wide * wide
        sums_lane[...] += squares[:, 0:128] + squares[:, 128:256] + squares[:, 256:384] + squares[:, 384:512]
        return carry

    lax.fori_loop(0, 16, project, 0)
    scale = lax.rsqrt(jnp.sum(sums_lane[...], axis=1, keepdims=True) * (1.0 / 8192) + EPSILON)
    cos, sin = cosine[...], sine[...]
    for h in range(5):
        part = acc[:, h * HD:(h + 1) * HD] * scale
        qkv[:, h * HD:(h + 1) * HD] = (part * cos + pltpu.roll(part, 64, 1) * sin).astype(BF16)
    qkv[:, 640:768] = (acc[:, 640:768] * scale).astype(BF16)

    for t in range(4):
        first = max(t * 128 - 128, 0)
        keys = qkv[first:first + 256, 512:640]
        vals = qkv[first:first + 256, 640:768]
        row = lax.broadcasted_iota(jnp.int32, (128, 256), 0) + t * 128
        col = lax.broadcasted_iota(jnp.int32, (128, 256), 1) + first
        allowed = (col <= row) & (col >= row - offset_col[t * 128:(t + 1) * 128, :])
        for h in range(4):
            query = qkv[t * 128:(t + 1) * 128, h * HD:(h + 1) * HD]
            scores = lax.dot_general(query, keys, (((1,), (1,)), ((), ())), preferred_element_type=F32)
            scores = jnp.where(allowed, scores * (HD ** -0.5), -1e30)
            weight = jnp.exp(scores - jnp.max(scores, axis=1, keepdims=True))
            probs = (weight / jnp.sum(weight, axis=1, keepdims=True)).astype(BF16)
            att[tp, t * 128:(t + 1) * 128, h * HD:(h + 1) * HD] = dot(probs, vals).astype(BF16)

    a_rows = ROWS // A_PIECES
    attended = Gather(
        lambda index, p: att.at[index, pl.ds(p * a_rows, a_rows)], tp_of, tp_dev, A_PIECES, a_send, a_recv, True, False
    )
    for p in range(A_PIECES):
        attended.own(p)
    for p in range(2):
        w_out.across(p)
        w_out.line(0, p)
    for p in range(A_PIECES):
        attended.across(p)
        attended.line(0, p)
    for p in range(2):
        w_out.line(1, p)
        w_out.opposite(0, p)
    for p in range(A_PIECES):
        attended.opposite(0, p)
    for p in range(2):
        w_out.opposite(1, p)
    for p in range(A_PIECES):
        attended.line(1, p)
    copied_on(w_out)
    for p in range(A_PIECES):
        attended.opposite(1, p)

    res[...] = hid[...].astype(F32)

    def output(k, carry):
        for c in range(2):
            res[:, c * 512:(c + 1) * 512] += dot(att[k], wog[c, k])
        return carry

    lax.fori_loop(0, 8, output, 0)

    def bucket(t, carry):
        slots = lax.broadcasted_iota(jnp.int32, (256, ROWS), 0) + t * 256
        chosen = jnp.where(slots == slot_row[...], 1.0, 0.0).astype(BF16)
        rows = dot(chosen, res[...].astype(BF16)).astype(BF16)
        outgoing[pl.ds(pl.multiple_of(t * 256, 256), 256)] = rows
        return carry

    lax.fori_loop(0, 4, bucket, 0)

    def place(index):
        return pl.ds(pl.multiple_of(index * CAP, CAP), CAP)

    for k in range(1, 16):
        to = lax.rem(zero + k, 16)
        send(outgoing.at[place(to)], incoming.at[place(zero)], x_send.at[k], x_recv.at[k], (to, tp))
    incoming[place(zero)] = outgoing[place(zero)]
    for k in range(1, 16):
        arrived(incoming.at[place(lax.rem(zero + 16 - k, 16))], x_recv.at[k])

    def unpack(t, carry):
        rows = lax.broadcasted_iota(jnp.int32, (256, 16 * CAP), 0) + t * 256
        chosen = jnp.where(rows == target_row[...], 1.0, 0.0).astype(BF16)
        out[pl.ds(pl.multiple_of(t * 256, 256), 256)] = dot(chosen, incoming[...]).astype(BF16)
        return carry

    lax.fori_loop(0, 2, unpack, 0)

    squares = jnp.zeros((ROWS, 128), F32)
    along = jnp.zeros((ROWS, 128), F32)
    for c in range(8):
        part = out[:, c * 128:(c + 1) * 128].astype(F32)
        squares = squares + part * part
        along = along + part * head_row[:, c * 128:(c + 1) * 128]
    sums[tp, 0:1, :] = jnp.sum(squares.T, axis=0, keepdims=True)
    sums[tp, 1:2, :] = jnp.sum(along.T, axis=0, keepdims=True)
    for k in range(1, 8):
        send(sums.at[tp], sums.at[tp], v_send.at[k], v_recv.at[k], (zero, lax.rem(tp + k, 8)))
    for k in range(1, 8):
        arrived(sums.at[lax.rem(tp + 8 - k, 8)], v_recv.at[k])
    total = sums[0]
    for k in range(1, 8):
        total = total + sums[k]
    val_out[...] = total[1:2] * lax.rsqrt(total[0:1] * (1.0 / 8192) + EPSILON)
    for copy in started:
        copy.wait_send()


STOP = 0


def shards(hidden_in, assignment, attn_gain, w_query, w_key, w_value_proj, w_out, value_head):
    zero = lax.axis_index("zero")
    tp = lax.axis_index("tp")
    scorers = jnp.arange(16, dtype=jnp.int32)
    rows = jnp.arange(ROWS, dtype=jnp.int32)
    places = jnp.arange(CAP, dtype=jnp.int32)
    blocks = assignment.reshape(16, ROWS)
    own = lax.dynamic_slice_in_dim(assignment, zero * ROWS, ROWS, 0)
    chosen = own[:, None] == scorers[None, :]
    first = jnp.min(jnp.where(chosen, rows[:, None], ROWS), axis=0)
    offset = rows - jnp.sum(jnp.where(chosen, first[None, :], 0), axis=1)
    slot_row = (own * CAP + offset)[None, :]
    counts = jnp.sum((blocks == zero).astype(jnp.int32), axis=1)
    starts = jnp.sum(jnp.where(scorers[None, :] < scorers[:, None], counts[None, :], 0), axis=1)
    target = jnp.where(places[None, :] < counts[:, None], starts[:, None] + places[None, :], -1).reshape(1, 16 * CAP)
    frequency = ROPE_BASE ** (-2.0 * jnp.arange(HD // 2, dtype=F32) / HD)
    angles = offset.astype(F32)[:, None] * frequency[None, :]
    cosine, sine = jnp.cos(angles), jnp.sin(angles)
    cosine = jnp.concatenate([cosine, cosine], axis=1)
    sine = jnp.concatenate([-sine, sine], axis=1)
    gain_col = lax.dynamic_slice_in_dim(attn_gain, zero * ROWS, ROWS, 0).astype(F32)[:, None]
    head_row = lax.dynamic_slice_in_dim(value_head, tp * FEATURES, FEATURES, 0).astype(F32)[None, :]
    vmem = pl.BlockSpec(memory_space=pltpu.VMEM)
    dma = pltpu.SemaphoreType.DMA
    scored, values = pl.pallas_call(
        layer,
        out_shape=(jax.ShapeDtypeStruct((ROWS, FEATURES), BF16), jax.ShapeDtypeStruct((1, ROWS), F32)),
        in_specs=[vmem] * 12,
        out_specs=(vmem, vmem),
        scratch_shapes=[
            pltpu.VMEM((8, ROWS, FEATURES), BF16),
            pltpu.VMEM((16, ROWS, QKV), BF16),
            pltpu.VMEM((2, 8, ROWS, 512), BF16),
            pltpu.VMEM((8, ROWS, 512), BF16),
            pltpu.VMEM((16 * CAP, FEATURES), BF16),
            pltpu.VMEM((16 * CAP, FEATURES), BF16),
            pltpu.VMEM((ROWS, QKV), F32),
            pltpu.VMEM((ROWS, QKV), BF16),
            pltpu.VMEM((ROWS, FEATURES), F32),
            pltpu.VMEM((8, 8, ROWS), F32),
            pltpu.VMEM((ROWS, 128), F32),
            dma((7 * H_PIECES,)), dma((8, H_PIECES)),
            dma((15 * W_PIECES,)), dma((16, W_PIECES)),
            dma((30,)), dma((16, 2)),
            dma((8,)), dma((8,)),
            dma((7 * A_PIECES,)), dma((8, A_PIECES)),
            dma((16,)), dma((16,)),
            dma((8,)), dma((8,)),
            dma,
        ],
        compiler_params=pltpu.CompilerParams(
            collective_id=0, has_side_effects=True, vmem_limit_bytes=58 * 2**20
        ),
        name="layer",
    )(
        hidden_in, w_query, w_key, w_value_proj, w_out, gain_col, slot_row, target, offset[:, None], cosine, sine,
        head_row,
    )
    return scored, values.reshape(ROWS)


def solution(mesh):
    in_specs = (P("zero", "tp"), P(), P(), P("zero", "tp"), P("zero", "tp"), P("zero", "tp"), P("tp", "zero"), P())
    return jax.shard_map(
        shards, mesh=mesh, in_specs=in_specs, out_specs=(P("zero", "tp"), P("zero")), check_vma=False
    )
```

time: 523 us -> 205 us (0.39)
  waiting for transfers between devices: 417 us -> 0 us
  Pallas kernels: 0 us -> 191 us
  matrix products: 38.3 us -> 0 us
  between operations: 14.3 us -> 0.69 us
  blocking collectives: 13 us -> 0 us
  starting transfers between devices: 9.7 us -> 0 us
  other arithmetic: 14.7 us -> 5.99 us
  local copies, waits for them, and re-layouts: 12.2 us -> 5.34 us
    all_gather x5 -> x0, waiting for transfers between devices: 298 us -> none  [the longest x1 85.9 us: shards(): gathered = lax.all_gather(packed, 'tp', axis=1, tiled=True)]
    pallas_call x0 -> x1, Pallas kernels: none -> 191 us  [shards(): pl.pallas_call(layer, out_shape=(jax.ShapeDtypeStruct((ROWS, FEATURES), B...]
    reduce_scatter x1 -> x0, waiting for transfers between devices: 89.1 us -> none  [shards(): lax.psum_scatter(partial_out.astype(jnp.bfloat16), 'tp', scatter_dimensio...]
    dot_general x5 -> x0, matrix products: 38.3 us -> none  [the longest x2 18 us: add_rows(): return jnp.dot(normed, weight_piece, preferred_element_type=jnp.float32)]
    all_to_all x1 -> x0, waiting for transfers between devices: 27.8 us -> none  [shards(): lax.all_to_all(outgoing, 'zero', split_axis=0, concat_axis=0, tiled=True)]
    psum x1 -> x0, blocking collectives: 13 us -> none  [shards(): lax.psum((jnp.sum(residual * residual, axis=1), jnp.sum(residual * own_he...]
    all_to_all x1 -> x0, starting transfers between devices: 9.29 us -> none  [shards(): lax.all_to_all(outgoing, 'zero', split_axis=0, concat_axis=0, tiled=True)]
    reduce_sum x7 -> x3, other arithmetic: 9.12 us -> 0.33 us  [the longest x1 0.12 us: shards(): counts = jnp.sum((blocks == zero).astype(jnp.int32), axis=1)]
  transfers between devices with their start and end apart: 7 -> 0, of which waited for: 7 -> 0; matrix products, arithmetic and copies ran while one was open for 7% -> 0% of each run, Pallas kernels for 0% -> 0%
where the time goes in v1:
time: 205 us; the launch traced here: 203 us
  Pallas kernels  191 us (93%)
  other arithmetic  5.99 us (3%)
  local copies, waits for them, and re-layouts  5.34 us (3%)
    pallas_call x1, Pallas kernels, shards(): pl.pallas_call(layer, out_shape=(jax.ShapeDtypeStruct((ROWS, FEATURES), B...  191 us

profile of v1, /device:TPU:1, one launch (start us, length us, event | category | flops | bytes accessed | tf_op | source)
XLA Modules:
  0.0 203.3 jit_solution(14584510850905584108)
XLA Ops:
  0.6 0.0 copy-start
  0.7 0.8 dynamic_slice.10
  1.5 0.1 select_reduce_fusion.1
  1.6 0.1 select_reduce_fusion
  1.7 0.8 dynamic-slice_convert_fusion.1
  2.4 1.3 dynamic-slice_convert_fusion
  3.7 0.0 copy-done
  3.7 0.7 fusion.1
  4.4 0.1 reduce_sum.30
  4.5 0.1 select_reduce_fusion.2
  4.6 0.1 add_select_fusion
  4.7 0.7 select_n.38.target_row
  5.4 0.9 copy.13.gain_col
  6.2 0.1 copy.12
  6.4 0.7 iota_subtract_fusion.offset_col
  7.1 1.0 fusion
  8.1 1.0 pad_maximum_fusion
  9.2 191.3 %layer.1 = (bf16[512,1024]{1,0:T(8,128)(2,1)}, f32[1,512]{1,0:T(1,128)}) custom-call(bf16[512,1024]{1,0:T(8,128)(2,1)} %hid.1, bf16[512,512]{1,0:T(8,128)(2,1)} %wq.1, bf16[512,128]{1,0:T(8,128)(2,1)} %wk.1, bf16[512,128]{1,0:T(8,128)(2,1)} %wv.1, bf16[512,512]{1,0:T(8,128)(2,1)} %wo.1, f32[512,1]{1,0:T(8,128)} %copy.13.gain_col, s32[1,512]{1,0:T(1,128)} %bitcast.7, ...), custom_call_target="tpu_custom_call" | custom-call | tf_op jit(solution)/shard_map/layer/pallas_call | solution.py:401
  200.4 0.0 copy-start.1
  200.4 2.3 %copy.16 = bf16[512,1024]{1,0:T(8,128)(2,1)} copy(bf16[512,1024]{1,0:T(8,128)(2,1)} %get-tuple-element.15) | data formatting | bytes 2097152
  202.7 0.0 copy-done.1
  202.7 0.6 copy.17
  (3 shorter events, 0.0 us)
Async XLA Ops:
  0.6 3.1 %copy-start = (s32[8192]{0:T(1024)S(1)}, s32[8192]{0:T(1024)}, u32[]{:S(2)}) copy-start(s32[8192]{0:T(1024)} %param.9) | copy-start | bytes 98308
  200.4 2.3 %copy-start.1 = (f32[1,512]{1,0:T(1,128)S(1)}, f32[1,512]{1,0:T(1,128)}, u32[]{:S(2)}) copy-start(f32[1,512]{1,0:T(1,128)} %get-tuple-element.5) | copy-start | bytes 6148

commit v2 on v1

v2 whole, which is shorter than its diff:
```python
import jax
import jax.numpy as jnp
import numpy as np
from jax import lax
from jax.experimental import pallas as pl
from jax.experimental.pallas import tpu as pltpu
from jax.sharding import PartitionSpec as P

HD = 128
EPSILON = 1e-05
ROPE_BASE = 500000.0
MESH = pl.DeviceIdType.MESH
ROWS = 512
FEATURES = 1024
QKV = 768
CAP = 64
H_PIECES = 4
W_PIECES = 4
A_PIECES = 4
BF16 = jnp.bfloat16
F32 = jnp.float32


def dot(a, b):
    return jnp.dot(a, b, preferred_element_type=F32)


def layer(
    hid, assignment, gain, head, wq, wk, wv, wo, table,
    out, val_out,
    hg, wg, wog, att, outgoing, incoming, acc, qkv, res, sums, lanes, blocks, turns, runs, packed_values, got_values, dealt,
    h_send, h_recv, w_send, w_recv, o_send, o_recv, r_send, r_recv, a_send, a_recv,
    x_send, x_recv, v_send, v_recv, y_send, y_recv, q_send, q_recv,
):
    zero = lax.axis_index("zero")
    tp = lax.axis_index("tp")
    z = lax.div(zero, 4)
    xh = lax.rem(lax.div(zero, 2), 2)
    core = lax.rem(zero, 2)
    xl = lax.div(tp, 4)
    y = lax.rem(tp, 4)
    spot = lax.div(zero, 2)

    def tp_of(far, dy):
        other = lax.rem(xl + far, 2)
        return other * 4 + lax.rem(y + dy + 4, 4)

    def spot_of(far, dz):
        other = lax.rem(xh + far, 2)
        return lax.rem(z + dz + 4, 4) * 2 + other

    def tp_dev(far, dy):
        return (zero, tp_of(far, dy))

    def zero_dev(far, dz):
        return (spot_of(far, dz) * 2 + core, tp)

    sibling = (spot * 2 + (1 - core), tp)

    barrier = pltpu.get_barrier_semaphore()
    greeted = 0
    for k in range(1, 16):
        pl.semaphore_signal(barrier, inc=1, device_id=(lax.rem(zero + k, 16), tp), device_id_type=MESH)
        greeted += 1
    for k in range(1, 8):
        pl.semaphore_signal(barrier, inc=1, device_id=(zero, lax.rem(tp + k, 8)), device_id_type=MESH)
        greeted += 1
    diagonal = lax.broadcasted_iota(jnp.int32, (128, 128), 0) == lax.broadcasted_iota(jnp.int32, (128, 128), 1)
    own_rows = pl.ds(pl.multiple_of(core * 512, 512), 512)
    gains = gain[pl.ds(pl.multiple_of(zero * ROWS, ROWS), ROWS)].astype(F32).reshape(1, ROWS)
    for t in range(4):
        column = jnp.sum(jnp.where(diagonal, gains[:, t * 128:(t + 1) * 128], 0.0), axis=1, keepdims=True)
        here = pl.ds(pl.multiple_of(core * 512 + t * 128, 128), 128)
        there = pl.ds(t * 128, 128)
        wg[spot, here, 0:512] = (wq[there].astype(F32) * column).astype(BF16)
        wg[spot, here, 512:640] = (wk[there].astype(F32) * column).astype(BF16)
        wg[spot, here, 640:768] = (wv[there].astype(F32) * column).astype(BF16)

    pl.semaphore_wait(barrier, greeted)

    started = []

    def send(src, dst, send_sem, recv_sem, device):
        copy = pltpu.make_async_remote_copy(
            src_ref=src, dst_ref=dst, send_sem=send_sem, recv_sem=recv_sem, device_id=device, device_id_type=MESH
        )
        copy.start()
        started.append(copy)

    def arrived(ref, sem):
        pltpu.make_async_remote_copy(
            src_ref=ref, dst_ref=ref, send_sem=sem, recv_sem=sem, device_id=sibling, device_id_type=MESH
        ).wait_recv()

    class Gather:
        def __init__(self, block, index_of, device_of, pieces, send_sems, recv_sems, across_relay, copy_on):
            self.block, self.index_of, self.device_of, self.pieces = block, index_of, device_of, pieces
            self.send_sems, self.recv_sems = send_sems, recv_sems
            self.across_relay, self.copy_on = across_relay, copy_on
            self.count = 0

        def push(self, index, p, device, src=None):
            dst = self.block(index, p)
            send(dst if src is None else src, dst, self.send_sems.at[self.count], self.recv_sems.at[index, p], device)
            self.count += 1

        def wait(self, index, p):
            arrived(self.block(index, p), self.recv_sems.at[index, p])

        def on(self, index, p, src=None):
            if self.copy_on:
                self.push(index, p, sibling, src)

        def own(self, p, src=None):
            index = self.index_of(0, 0)
            self.push(index, p, self.device_of(1, 0), src)
            self.push(index, p, self.device_of(0, 1), src)
            self.push(index, p, self.device_of(0, -1), src)
            self.on(index, p, src)

        def across(self, p):
            index = self.index_of(1, 0)
            self.wait(index, p)
            self.push(index, p, self.device_of(0, 1))
            self.push(index, p, self.device_of(0, -1))
            self.on(index, p)

        def line(self, far, p):
            last = self.pieces - 1 - p
            below, above = self.index_of(far, -1), self.index_of(far, 1)
            relayed = (far == 0 or not self.across_relay) and p < self.pieces // 2
            self.wait(below, p)
            if relayed:
                self.push(below, p, self.device_of(0, 1))
            self.wait(above, last)
            if relayed:
                self.push(above, last, self.device_of(0, -1))
            self.on(below, p)
            self.on(above, last)

        def opposite(self, far, step):
            p = step // 2 if step % 2 == 0 else self.pieces - 1 - step // 2
            index = self.index_of(far, 2)
            self.wait(index, p)
            if far == 0 and self.across_relay:
                self.push(index, p, self.device_of(1, 0))
            self.on(index, p)

    def copied_on(gather):
        for far in range(2):
            for d in (0, 1, -1, 2):
                for p in range(gather.pieces):
                    gather.wait(spot_of(far, d) * 2 + (1 - core), p)

    h_rows = ROWS // H_PIECES
    hidden = Gather(
        lambda index, p: hg.at[index, pl.ds(p * h_rows, h_rows)], tp_of, tp_dev, H_PIECES, h_send, h_recv, True, False
    )
    w_rows = ROWS // W_PIECES
    weights = Gather(
        lambda index, p: wg.at[
            lax.div(index, 2), pl.ds(pl.multiple_of(lax.rem(index, 2) * 512 + p * w_rows, w_rows), w_rows)
        ],
        lambda far, dz: spot_of(far, dz) * 2 + core, zero_dev, W_PIECES, w_send, w_recv, False, True,
    )
    w_out = Gather(
        lambda index, p: wog.at[
            lax.rem(index, 2), pl.ds(p * 4, 4), pl.ds(pl.multiple_of(lax.div(index, 2) * 64, 64), 64)
        ],
        lambda far, dz: spot_of(far, dz) * 2 + core, zero_dev, 2, o_send, o_recv, False, True,
    )
    a_rows = ROWS // A_PIECES
    attended = Gather(
        lambda index, p: att.at[index, pl.ds(p * a_rows, a_rows)], tp_of, tp_dev, A_PIECES, a_send, a_recv, True, False
    )
    for p in range(4):
        hidden.own(p, hid.at[pl.ds(p * h_rows, h_rows)])
        weights.own(p)
    hg[tp] = hid[...]

    own = assignment[pl.ds(pl.multiple_of(zero * ROWS, ROWS), ROWS)].reshape(1, ROWS)
    row_id = lax.broadcasted_iota(jnp.int32, (ROWS, ROWS), 0)
    col_id = lax.broadcasted_iota(jnp.int32, (ROWS, ROWS), 1)
    equal = row_id == col_id
    own_col = jnp.sum(jnp.where(equal, own, 0), axis=1, keepdims=True)
    offset = jnp.sum(jnp.where((own == own_col) & (col_id < row_id), 1, 0), axis=1, keepdims=True)
    offset_row = jnp.sum(jnp.where(equal, offset, 0), axis=0, keepdims=True)
    runs[0:1, 0:ROWS] = own * CAP + offset_row
    runs[1:2, 0:ROWS] = own
    for k in range(16):
        blocks[k:k + 1, :] = assignment[pl.ds(k * ROWS, ROWS)].reshape(1, ROWS)
    counts = jnp.sum(jnp.where(blocks[...] == zero, 1, 0), axis=1, keepdims=True)
    row_16 = lax.broadcasted_iota(jnp.int32, (16, 16), 0)
    col_16 = lax.broadcasted_iota(jnp.int32, (16, 16), 1)
    counts_row = jnp.sum(jnp.where(row_16 == col_16, counts, 0), axis=0, keepdims=True)
    starts = jnp.sum(jnp.where(col_16 < row_16, counts_row, 0), axis=1, keepdims=True)
    slot = lax.broadcasted_iota(jnp.int32, (16, 16 * CAP), 1)
    place_in = slot - lax.broadcasted_iota(jnp.int32, (16, 16 * CAP), 0) * CAP
    filled = (place_in >= 0) & (place_in < CAP) & (place_in < counts)
    runs[2:3, :] = jnp.sum(jnp.where(filled, starts + place_in + 1, 0), axis=0, keepdims=True) - 1
    place_row = lax.broadcasted_iota(jnp.int32, (16, ROWS), 1)
    from_block = (place_row >= starts) & (place_row < starts + counts)
    runs[3:4, 0:ROWS] = jnp.sum(jnp.where(from_block, place_row - starts, 0), axis=0, keepdims=True)
    runs[4:5, 0:ROWS] = jnp.sum(
        jnp.where(from_block, lax.broadcasted_iota(jnp.int32, (16, ROWS), 0), 0), axis=0, keepdims=True
    )
    in_run = jnp.where(offset == lax.broadcasted_iota(jnp.int32, (ROWS, 64), 1), 1.0, 0.0)
    turns[:, 0:256] = jnp.dot(in_run, table[...], precision=lax.Precision.HIGHEST, preferred_element_type=F32)
    turns[:, 256:384] = jnp.broadcast_to(offset.astype(F32), (ROWS, 128))
    acc[...] = jnp.zeros_like(acc)
    lanes[...] = jnp.zeros_like(lanes)

    for p in range(2):
        hidden.line(0, p)
        weights.line(0, p)
    for p in range(4):
        hidden.across(p)
        hidden.opposite(0, p)
        weights.across(p)
    for p in range(2, 4):
        hidden.line(0, p)
        weights.line(0, p)
    for p in range(4):
        weights.line(1, p)
        weights.opposite(0, p)

    my_rows = pl.ds(pl.multiple_of(spot * 64, 64), 64)
    for k in range(1, 8):
        slot = lax.rem(spot + k, 8)
        rows = pl.ds(pl.multiple_of(slot * 64, 64), 64)
        send(wo.at[rows], dealt.at[spot], r_send.at[k], r_recv.at[k], (slot * 2 + core, tp))
    dealt[spot] = wo[my_rows]
    for p in range(4):
        weights.opposite(1, p)
    copied_on(weights)

    def project(index):
        block = hg[index]
        acc[...] += dot(block, wg[index])
        total = lanes[...]
        for c in range(8):
            wide = block[:, c * 128:(c + 1) * 128].astype(F32)
            total = total + wide * wide
        lanes[...] = total

    project(tp)
    project(tp_of(0, 1))
    project(tp_of(0, -1))
    for k in range(1, 8):
        arrived(dealt.at[lax.rem(spot + 8 - k, 8)], r_recv.at[k])
    for k in range(1, 8):
        to = lax.rem(tp + k, 8)
        send(dealt.at[to], wog.at[core, tp, my_rows], q_send.at[k], q_recv.at[k], (zero, to))
    wog[core, tp, my_rows] = dealt[tp]
    project(tp_of(0, 2))
    project(tp_of(1, 0))
    for p in range(4):
        hidden.line(1, p)
    project(tp_of(1, 1))
    project(tp_of(1, -1))
    for p in range(4):
        hidden.opposite(1, p)
    project(tp_of(1, 2))
    for k in range(1, 8):
        arrived(wog.at[core, lax.rem(tp + 8 - k, 8), my_rows], q_recv.at[k])
    for p in range(2):
        w_out.own(p)
    scale = lax.rsqrt(jnp.sum(lanes[...], axis=1, keepdims=True) * (1.0 / 8192) + EPSILON)
    cos, sin = turns[:, 0:128], turns[:, 128:256]
    for h in range(5):
        part = acc[:, h * HD:(h + 1) * HD] * scale
        qkv[:, h * HD:(h + 1) * HD] = (part * cos + pltpu.roll(part, 64, 1) * sin).astype(BF16)
    qkv[:, 640:768] = (acc[:, 640:768] * scale).astype(BF16)

    for t in range(4):
        first = max(t * 128 - 128, 0)
        keys = qkv[first:first + 256, 512:640]
        vals = qkv[first:first + 256, 640:768]
        row = lax.broadcasted_iota(jnp.int32, (128, 256), 0) + t * 128
        col = lax.broadcasted_iota(jnp.int32, (128, 256), 1) + first
        back = turns[t * 128:(t + 1) * 128, 256:384].astype(jnp.int32)
        allowed = (col <= row) & (col >= row - jnp.concatenate([back, back], axis=1))
        for h in range(4):
            query = qkv[t * 128:(t + 1) * 128, h * HD:(h + 1) * HD]
            scores = lax.dot_general(query, keys, (((1,), (1,)), ((), ())), preferred_element_type=F32)
            scores = jnp.where(allowed, scores * (HD ** -0.5), -1e30)
            weight = jnp.exp(scores - jnp.max(scores, axis=1, keepdims=True))
            probs = (weight / jnp.sum(weight, axis=1, keepdims=True)).astype(BF16)
            att[tp, t * 128:(t + 1) * 128, h * HD:(h + 1) * HD] = dot(probs, vals).astype(BF16)
        attended.own(t)

    w_out.line(0, 0)
    for p in range(2):
        attended.line(0, p)
    for p in range(2):
        attended.across(p)
        attended.opposite(0, p)
        w_out.across(p)
    for p in range(2, 4):
        attended.across(p)
        attended.opposite(0, p)
    w_out.line(0, 1)
    for p in range(2, 4):
        attended.line(0, p)
    for p in range(2):
        w_out.line(1, p)
        w_out.opposite(0, p)
    for step in range(2):
        w_out.opposite(1, step)
    copied_on(w_out)

    res[...] = hid[...].astype(F32)

    def output(index):
        for c in range(2):
            res[:, c * 512:(c + 1) * 512] += dot(att[index], wog[c, index])

    output(tp)
    output(tp_of(0, 1))
    output(tp_of(0, -1))
    output(tp_of(0, 2))
    output(tp_of(1, 0))
    for p in range(4):
        attended.line(1, p)
    output(tp_of(1, 1))
    output(tp_of(1, -1))
    for step in range(4):
        attended.opposite(1, step)
    output(tp_of(1, 2))

    def place(index):
        return pl.ds(pl.multiple_of(index * CAP, CAP), CAP)

    rounded = res[...].astype(BF16)
    for t in (2, 1, 3, 0):
        slots = lax.rem(lax.broadcasted_iota(jnp.int32, (256, ROWS), 0) + (zero * CAP + t * 256), 16 * CAP)
        chosen = jnp.where(slots == runs[0:1, 0:ROWS], 1.0, 0.0).astype(BF16)
        outgoing[t * 256:(t + 1) * 256, :] = dot(chosen, rounded).astype(BF16)
        for k in range(t * 4, t * 4 + 4):
            if k > 0:
                to = lax.rem(zero + k, 16)
                send(
                    outgoing.at[pl.ds(k * CAP, CAP)], incoming.at[place(zero)], x_send.at[k], x_recv.at[k], (to, tp)
                )
    incoming[place(zero)] = outgoing[0:CAP]

    squares = jnp.zeros((ROWS, 128), F32)
    along = jnp.zeros((ROWS, 128), F32)
    heads = head[pl.ds(pl.multiple_of(tp * FEATURES, FEATURES), FEATURES)].astype(F32).reshape(1, FEATURES)
    for c in range(8):
        part = res[:, c * 128:(c + 1) * 128]
        weight = heads[:, c * 128:(c + 1) * 128]
        squares = squares + part * part
        along = along + part * weight
    sums[tp, 0:1, :] = jnp.sum(squares.T, axis=0, keepdims=True)
    sums[tp, 1:2, :] = jnp.sum(along.T, axis=0, keepdims=True)
    for k in range(1, 8):
        send(sums.at[tp], sums.at[tp], v_send.at[k], v_recv.at[k], (zero, lax.rem(tp + k, 8)))
    for k in range(1, 8):
        arrived(sums.at[lax.rem(tp + 8 - k, 8)], v_recv.at[k])
    total = sums[0]
    for k in range(1, 8):
        total = total + sums[k]
    value = total[1:2] * lax.rsqrt(total[0:1] * (1.0 / 8192) + EPSILON)
    to_scorer = jnp.where(lax.broadcasted_iota(jnp.int32, (16, ROWS), 0) == runs[1:2, 0:ROWS], value, 0.0)
    back = turns[:, 256:384].astype(jnp.int32)
    in_place = jnp.where(back == lax.broadcasted_iota(jnp.int32, (ROWS, 128), 1), 1.0, 0.0)
    bucketed = jnp.dot(to_scorer, in_place, precision=lax.Precision.HIGHEST, preferred_element_type=F32)
    packed_values[...] = jnp.broadcast_to(bucketed[:, None, :], (16, 8, 128))
    for k in range(1, 16):
        to = lax.rem(zero + k, 16)
        send(packed_values.at[to], got_values.at[zero], y_send.at[k], y_recv.at[k], (to, tp))
    got_values[zero] = packed_values[zero]
    for k in range(1, 16):
        arrived(got_values.at[lax.rem(zero + 16 - k, 16)], y_recv.at[k])
    at_place = jnp.where(lax.broadcasted_iota(jnp.int32, (128, ROWS), 0) == runs[3:4, 0:ROWS], 1.0, 0.0)
    spread = jnp.dot(got_values[:, 0, :], at_place, precision=lax.Precision.HIGHEST, preferred_element_type=F32)
    mine = lax.broadcasted_iota(jnp.int32, (16, ROWS), 0) == runs[4:5, 0:ROWS]
    val_out[...] = jnp.sum(jnp.where(mine, spread, 0.0), axis=0, keepdims=True)

    for k in range(1, 16):
        arrived(incoming.at[place(lax.rem(zero + 16 - k, 16))], x_recv.at[k])
    for t in range(2):
        rows = lax.broadcasted_iota(jnp.int32, (256, 16 * CAP), 0) + t * 256
        chosen = jnp.where(rows == runs[2:3, :], 1.0, 0.0).astype(BF16)
        out[t * 256:(t + 1) * 256, :] = dot(chosen, incoming[...]).astype(BF16)
    for copy in started:
        copy.wait_send()


def rotary_table():
    angles = np.arange(CAP)[:, None] * ROPE_BASE ** (-2.0 * np.arange(HD // 2) / HD)[None, :]
    cosine, sine = np.cos(angles), np.sin(angles)
    return np.concatenate([cosine, cosine, -sine, sine], axis=1).astype(np.float32)


def shards(hidden_in, assignment, attn_gain, w_query, w_key, w_value_proj, w_out, value_head):
    vmem = pl.BlockSpec(memory_space=pltpu.VMEM)
    dma = pltpu.SemaphoreType.DMA
    scored, values = pl.pallas_call(
        layer,
        out_shape=(jax.ShapeDtypeStruct((ROWS, FEATURES), BF16), jax.ShapeDtypeStruct((1, ROWS), F32)),
        in_specs=[vmem] * 9,
        out_specs=(vmem, vmem),
        scratch_shapes=[
            pltpu.VMEM((8, ROWS, FEATURES), BF16),
            pltpu.VMEM((8, 2 * ROWS, QKV), BF16),
            pltpu.VMEM((2, 8, ROWS, 512), BF16),
            pltpu.VMEM((8, ROWS, 512), BF16),
            pltpu.VMEM((16 * CAP, FEATURES), BF16),
            pltpu.VMEM((16 * CAP, FEATURES), BF16),
            pltpu.VMEM((ROWS, QKV), F32),
            pltpu.VMEM((ROWS, QKV), BF16),
            pltpu.VMEM((ROWS, FEATURES), F32),
            pltpu.VMEM((8, 8, ROWS), F32),
            pltpu.VMEM((ROWS, 128), F32),
            pltpu.VMEM((16, ROWS), jnp.int32),
            pltpu.VMEM((ROWS, 384), F32),
            pltpu.VMEM((8, 16 * CAP), jnp.int32),
            pltpu.VMEM((16, 8, 128), F32),
            pltpu.VMEM((16, 8, 128), F32),
            pltpu.VMEM((8, 64, 512), BF16),
            dma((7 * H_PIECES,)), dma((8, H_PIECES)),
            dma((15 * W_PIECES,)), dma((16, W_PIECES)),
            dma((30,)), dma((16, 2)),
            dma((8,)), dma((8,)),
            dma((7 * A_PIECES,)), dma((8, A_PIECES)),
            dma((16,)), dma((16,)),
            dma((8,)), dma((8,)),
            dma((16,)), dma((16,)),
            dma((8,)), dma((8,)),
        ],
        compiler_params=pltpu.CompilerParams(
            collective_id=0, has_side_effects=True, vmem_limit_bytes=58 * 2**20
        ),
        name="layer",
    )(
        hidden_in, assignment, attn_gain, value_head, w_query, w_key, w_value_proj, w_out,
        jnp.asarray(rotary_table()),
    )
    return scored, values.reshape(ROWS)


def solution(mesh):
    in_specs = (P("zero", "tp"), P(), P(), P("zero", "tp"), P("zero", "tp"), P("zero", "tp"), P("tp", "zero"), P())
    return jax.shard_map(
        shards, mesh=mesh, in_specs=in_specs, out_specs=(P("zero", "tp"), P("zero")), check_vma=False
    )
```

time: 205 us -> 178 us (0.87)
  Pallas kernels: 191 us -> 175 us
  other arithmetic: 5.99 us -> 0 us
  local copies, waits for them, and re-layouts: 5.34 us -> 2.85 us
    pallas_call x1, Pallas kernels: 191 us -> 175 us  [shards(): pl.pallas_call(layer, out_shape=(jax.ShapeDtypeStruct((ROWS, FEATURES), B...]
where the time goes in v2:
time: 178 us
  Pallas kernels  175 us (98%)
  local copies, waits for them, and re-layouts  2.85 us (2%)
    pallas_call x1, Pallas kernels, shards(): pl.pallas_call(layer, out_shape=(jax.ShapeDtypeStruct((ROWS, FEATURES), B...  175 us

profile of v2, /device:TPU:1, one launch (start us, length us, event | category | flops | bytes accessed | tf_op | source)
XLA Modules:
  0.0 178.2 jit_solution(12751507079867904559)
XLA Ops:
  0.6 174.7 %layer.1 = (bf16[512,1024]{1,0:T(8,128)(2,1)}, f32[1,512]{1,0:T(1,128)}) custom-call(bf16[512,1024]{1,0:T(8,128)(2,1)} %hid.1, s32[8192]{0:T(1024)} %assignment.1, bf16[8192]{0:T(1024)(128)(2,1)} %gain.1, bf16[8192]{0:T(1024)(128)(2,1)} %head.1, bf16[512,512]{1,0:T(8,128)(2,1)} %wq.1, bf16[512,128]{1,0:T(8,128)(2,1)} %wk.1, bf16[512,128]{1,0:T(8,128)(2,1)} %wv.1, ...), custom_call_target="tpu_custom_call" | custom-call | tf_op jit(solution)/shard_map/layer/pallas_call | solution.py:400
  175.3 0.0 copy-start
  175.3 2.3 %copy.13 = bf16[512,1024]{1,0:T(8,128)(2,1)} copy(bf16[512,1024]{1,0:T(8,128)(2,1)} %get-tuple-element.8) | data formatting | bytes 2097152
  177.6 0.0 copy-done
  177.6 0.6 copy.14
Async XLA Ops:
  175.3 2.3 %copy-start = (f32[1,512]{1,0:T(1,128)S(1)}, f32[1,512]{1,0:T(1,128)}, u32[]{:S(2)}) copy-start(f32[1,512]{1,0:T(1,128)} %get-tuple-element.5) | copy-start | bytes 6148

commit v3 on v2

--- a/solution.py
+++ b/solution.py
@@ -17,6 +17,7 @@
 H_PIECES = 4
 W_PIECES = 4
 A_PIECES = 4
+A_ENDS = 1
 BF16 = jnp.bfloat16
 F32 = jnp.float32
 
@@ -28,7 +29,7 @@
 def layer(
     hid, assignment, gain, head, wq, wk, wv, wo, table,
     out, val_out,
-    hg, wg, wog, att, outgoing, incoming, acc, qkv, res, sums, lanes, blocks, turns, runs, packed_values, got_values, dealt,
+    hg, wg, wog, att, outgoing, incoming, rounded, acc, qkv, res, sums, lanes, blocks, turns, runs, packed_values, got_values, dealt,
     h_send, h_recv, w_send, w_recv, o_send, o_recv, r_send, r_recv, a_send, a_recv,
     x_send, x_recv, v_send, v_recv, y_send, y_recv, q_send, q_recv,
 ):
@@ -93,10 +94,10 @@
         ).wait_recv()
 
     class Gather:
-        def __init__(self, block, index_of, device_of, pieces, send_sems, recv_sems, across_relay, copy_on):
+        def __init__(self, block, index_of, device_of, pieces, send_sems, recv_sems, across_relay, copy_on, ends=0):
             self.block, self.index_of, self.device_of, self.pieces = block, index_of, device_of, pieces
             self.send_sems, self.recv_sems = send_sems, recv_sems
-            self.across_relay, self.copy_on = across_relay, copy_on
+            self.across_relay, self.copy_on, self.ends = across_relay, copy_on, ends
             self.count = 0
 
         def push(self, index, p, device, src=None):
@@ -129,6 +130,8 @@
             last = self.pieces - 1 - p
             below, above = self.index_of(far, -1), self.index_of(far, 1)
             relayed = (far == 0 or not self.across_relay) and p < self.pieces // 2
+            if far == 1 and self.across_relay:
+                relayed = p < self.ends
             self.wait(below, p)
             if relayed:
                 self.push(below, p, self.device_of(0, 1))
@@ -142,14 +145,14 @@
             p = step // 2 if step % 2 == 0 else self.pieces - 1 - step // 2
             index = self.index_of(far, 2)
             self.wait(index, p)
-            if far == 0 and self.across_relay:
+            if far == 0 and self.across_relay and self.ends <= p < self.pieces - self.ends:
                 self.push(index, p, self.device_of(1, 0))
             self.on(index, p)
 
-    def copied_on(gather):
+    def copied_on(gather, pieces):
         for far in range(2):
             for d in (0, 1, -1, 2):
-                for p in range(gather.pieces):
+                for p in pieces:
                     gather.wait(spot_of(far, d) * 2 + (1 - core), p)
 
     h_rows = ROWS // H_PIECES
@@ -165,13 +168,14 @@
     )
     w_out = Gather(
         lambda index, p: wog.at[
-            lax.rem(index, 2), pl.ds(p * 4, 4), pl.ds(pl.multiple_of(lax.div(index, 2) * 64, 64), 64)
+            lax.rem(index, 2), pl.ds(p // 2 * 4, 4), pl.ds(pl.multiple_of(lax.div(index, 2) * 64, 64), 64),
+            pl.ds(0 if p in (0, 3) else 256, 256),
         ],
-        lambda far, dz: spot_of(far, dz) * 2 + core, zero_dev, 2, o_send, o_recv, False, True,
+        lambda far, dz: spot_of(far, dz) * 2 + core, zero_dev, 4, o_send, o_recv, False, True,
     )
     a_rows = ROWS // A_PIECES
     attended = Gather(
-        lambda index, p: att.at[index, pl.ds(p * a_rows, a_rows)], tp_of, tp_dev, A_PIECES, a_send, a_recv, True, False
+        lambda index, p: att.at[index, pl.ds(p * a_rows, a_rows)], tp_of, tp_dev, A_PIECES, a_send, a_recv, True, False, A_ENDS
     )
     for p in range(4):
         hidden.own(p, hid.at[pl.ds(p * h_rows, h_rows)])
@@ -232,7 +236,7 @@
     dealt[spot] = wo[my_rows]
     for p in range(4):
         weights.opposite(1, p)
-    copied_on(weights)
+    copied_on(weights, range(4))
 
     def project(index):
         block = hg[index]
@@ -263,7 +267,7 @@
     project(tp_of(1, 2))
     for k in range(1, 8):
         arrived(wog.at[core, lax.rem(tp + 8 - k, 8), my_rows], q_recv.at[k])
-    for p in range(2):
+    for p in (0, 3, 1, 2):
         w_out.own(p)
     scale = lax.rsqrt(jnp.sum(lanes[...], axis=1, keepdims=True) * (1.0 / 8192) + EPSILON)
     cos, sin = turns[:, 0:128], turns[:, 128:256]
@@ -292,70 +296,91 @@
     w_out.line(0, 0)
     for p in range(2):
         attended.line(0, p)
+    w_out.across(0)
+    w_out.across(3)
     for p in range(2):
         attended.across(p)
         attended.opposite(0, p)
-        w_out.across(p)
+    w_out.line(1, 0)
+    w_out.line(0, 1)
     for p in range(2, 4):
         attended.across(p)
         attended.opposite(0, p)
-    w_out.line(0, 1)
+    w_out.across(1)
+    w_out.across(2)
+    for p in range(A_ENDS):
+        attended.line(1, p)
     for p in range(2, 4):
         attended.line(0, p)
-    for p in range(2):
-        w_out.line(1, p)
-        w_out.opposite(0, p)
+    w_out.line(1, 1)
+    w_out.line(0, 3)
+    w_out.line(1, 3)
     for step in range(2):
+        w_out.opposite(0, step)
         w_out.opposite(1, step)
-    copied_on(w_out)
+    copied_on(w_out, (0, 3))
+
+    def output(h, index):
+        for c in range(2):
+            columns = pl.ds(c * 512 + h * 256, 256)
+            res[:, columns] += dot(att[index], wog[c, index, :, h * 256:(h + 1) * 256])
+
+    def place(index):
+        return pl.ds(pl.multiple_of(index * CAP, CAP), CAP)
+
+    def scatter(h):
+        for c in range(2):
+            rounded[:, c * 256:(c + 1) * 256] = res[:, c * 512 + h * 256:c * 512 + (h + 1) * 256].astype(BF16)
+        for t in (2, 1, 3, 0):
+            slots = lax.rem(lax.broadcasted_iota(jnp.int32, (256, ROWS), 0) + (zero * CAP + t * 256), 16 * CAP)
+            chosen = jnp.where(slots == runs[0:1, 0:ROWS], 1.0, 0.0).astype(BF16)
+            outgoing[h, t * 256:(t + 1) * 256, :] = dot(chosen, rounded[...]).astype(BF16)
+            for k in range(t * 4, t * 4 + 4):
+                if k > 0:
+                    to = lax.rem(zero + k, 16)
+                    send(
+                        outgoing.at[h, pl.ds(k * CAP, CAP)], incoming.at[h, place(zero)],
+                        x_send.at[h, k], x_recv.at[h, k], (to, tp),
+                    )
+        incoming[h, place(zero)] = outgoing[h, 0:CAP]
 
     res[...] = hid[...].astype(F32)
-
-    def output(index):
-        for c in range(2):
-            res[:, c * 512:(c + 1) * 512] += dot(att[index], wog[c, index])
-
-    output(tp)
-    output(tp_of(0, 1))
-    output(tp_of(0, -1))
-    output(tp_of(0, 2))
-    output(tp_of(1, 0))
-    for p in range(4):
+    output(0, tp)
+    output(0, tp_of(0, 1))
+    output(0, tp_of(0, -1))
+    output(0, tp_of(0, 2))
+    output(0, tp_of(1, 0))
+    for p in range(A_ENDS, 4):
         attended.line(1, p)
-    output(tp_of(1, 1))
-    output(tp_of(1, -1))
+    output(0, tp_of(1, 1))
+    output(0, tp_of(1, -1))
     for step in range(4):
         attended.opposite(1, step)
-    output(tp_of(1, 2))
-
-    def place(index):
-        return pl.ds(pl.multiple_of(index * CAP, CAP), CAP)
-
-    rounded = res[...].astype(BF16)
-    for t in (2, 1, 3, 0):
-        slots = lax.rem(lax.broadcasted_iota(jnp.int32, (256, ROWS), 0) + (zero * CAP + t * 256), 16 * CAP)
-        chosen = jnp.where(slots == runs[0:1, 0:ROWS], 1.0, 0.0).astype(BF16)
-        outgoing[t * 256:(t + 1) * 256, :] = dot(chosen, rounded).astype(BF16)
-        for k in range(t * 4, t * 4 + 4):
-            if k > 0:
-                to = lax.rem(zero + k, 16)
-                send(
-                    outgoing.at[pl.ds(k * CAP, CAP)], incoming.at[place(zero)], x_send.at[k], x_recv.at[k], (to, tp)
-                )
-    incoming[place(zero)] = outgoing[0:CAP]
+    output(0, tp_of(1, 2))
+    scatter(0)
+
+    w_out.line(0, 2)
+    w_out.line(1, 2)
+    for step in range(2, 4):
+        w_out.opposite(0, step)
+        w_out.opposite(1, step)
+    copied_on(w_out, (1, 2))
+    for far, d in ((0, 0), (0, 1), (0, -1), (0, 2), (1, 0), (1, 1), (1, -1), (1, 2)):
+        output(1, tp_of(far, d))
 
     squares = jnp.zeros((ROWS, 128), F32)
     along = jnp.zeros((ROWS, 128), F32)
     heads = head[pl.ds(pl.multiple_of(tp * FEATURES, FEATURES), FEATURES)].astype(F32).reshape(1, FEATURES)
     for c in range(8):
         part = res[:, c * 128:(c + 1) * 128]
-        weight = heads[:, c * 128:(c + 1) * 128]
         squares = squares + part * part
-        along = along + part * weight
+        along = along + part * heads[:, c * 128:(c + 1) * 128]
     sums[tp, 0:1, :] = jnp.sum(squares.T, axis=0, keepdims=True)
     sums[tp, 1:2, :] = jnp.sum(along.T, axis=0, keepdims=True)
     for k in range(1, 8):
         send(sums.at[tp], sums.at[tp], v_send.at[k], v_recv.at[k], (zero, lax.rem(tp + k, 8)))
+    scatter(1)
+
     for k in range(1, 8):
         arrived(sums.at[lax.rem(tp + 8 - k, 8)], v_recv.at[k])
     total = sums[0]
@@ -378,12 +403,16 @@
     mine = lax.broadcasted_iota(jnp.int32, (16, ROWS), 0) == runs[4:5, 0:ROWS]
     val_out[...] = jnp.sum(jnp.where(mine, spread, 0.0), axis=0, keepdims=True)
 
-    for k in range(1, 16):
-        arrived(incoming.at[place(lax.rem(zero + 16 - k, 16))], x_recv.at[k])
-    for t in range(2):
-        rows = lax.broadcasted_iota(jnp.int32, (256, 16 * CAP), 0) + t * 256
-        chosen = jnp.where(rows == runs[2:3, :], 1.0, 0.0).astype(BF16)
-        out[t * 256:(t + 1) * 256, :] = dot(chosen, incoming[...]).astype(BF16)
+    for h in range(2):
+        for k in range(1, 16):
+            arrived(incoming.at[h, place(lax.rem(zero + 16 - k, 16))], x_recv.at[h, k])
+        for t in range(2):
+            rows = lax.broadcasted_iota(jnp.int32, (256, 16 * CAP), 0) + t * 256
+            chosen = jnp.where(rows == runs[2:3, :], 1.0, 0.0).astype(BF16)
+            found = dot(chosen, incoming[h]).astype(BF16)
+            for c in range(2):
+                columns = pl.ds(c * 512 + h * 256, 256)
+                out[t * 256:(t + 1) * 256, columns] = found[:, c * 256:(c + 1) * 256]
     for copy in started:
         copy.wait_send()
 
@@ -407,8 +436,9 @@
             pltpu.VMEM((8, 2 * ROWS, QKV), BF16),
             pltpu.VMEM((2, 8, ROWS, 512), BF16),
             pltpu.VMEM((8, ROWS, 512), BF16),
-            pltpu.VMEM((16 * CAP, FEATURES), BF16),
-            pltpu.VMEM((16 * CAP, FEATURES), BF16),
+            pltpu.VMEM((2, 16 * CAP, 512), BF16),
+            pltpu.VMEM((2, 16 * CAP, 512), BF16),
+            pltpu.VMEM((ROWS, 512), BF16),
             pltpu.VMEM((ROWS, QKV), F32),
             pltpu.VMEM((ROWS, QKV), BF16),
             pltpu.VMEM((ROWS, FEATURES), F32),
@@ -422,10 +452,10 @@
             pltpu.VMEM((8, 64, 512), BF16),
             dma((7 * H_PIECES,)), dma((8, H_PIECES)),
             dma((15 * W_PIECES,)), dma((16, W_PIECES)),
-            dma((30,)), dma((16, 2)),
+            dma((60,)), dma((16, 4)),
             dma((8,)), dma((8,)),
             dma((7 * A_PIECES,)), dma((8, A_PIECES)),
-            dma((16,)), dma((16,)),
+            dma((2, 16)), dma((2, 16)),
             dma((8,)), dma((8,)),
             dma((16,)), dma((16,)),
             dma((8,)), dma((8,)),

time: 178 us -> 169 us (0.949)
  Pallas kernels: 175 us -> 164 us
    pallas_call x1, Pallas kernels: 175 us -> 164 us  [shards(): pl.pallas_call(layer, out_shape=(jax.ShapeDtypeStruct((ROWS, FEATURES), B...]
where the time goes in v3:
time: 169 us; the launch traced here: 168 us
  Pallas kernels  164 us (97%)
  local copies, waits for them, and re-layouts  2.85 us (2%)
    pallas_call x1, Pallas kernels, shards(): pl.pallas_call(layer, out_shape=(jax.ShapeDtypeStruct((ROWS, FEATURES), B...  164 us

profile of v3, /device:TPU:1, one launch (start us, length us, event | category | flops | bytes accessed | tf_op | source)
XLA Modules:
  0.0 167.6 jit_solution(2171746087220904699)
XLA Ops:
  0.6 164.1 %layer.1 = (bf16[512,1024]{1,0:T(8,128)(2,1)}, f32[1,512]{1,0:T(1,128)}) custom-call(bf16[512,1024]{1,0:T(8,128)(2,1)} %hid.1, s32[8192]{0:T(1024)} %assignment.1, bf16[8192]{0:T(1024)(128)(2,1)} %gain.1, bf16[8192]{0:T(1024)(128)(2,1)} %head.1, bf16[512,512]{1,0:T(8,128)(2,1)} %wq.1, bf16[512,128]{1,0:T(8,128)(2,1)} %wk.1, bf16[512,128]{1,0:T(8,128)(2,1)} %wv.1, ...), custom_call_target="tpu_custom_call" | custom-call | tf_op jit(solution)/shard_map/layer/pallas_call | solution.py:429
  164.8 0.0 copy-start
  164.8 2.3 %copy.13 = bf16[512,1024]{1,0:T(8,128)(2,1)} copy(bf16[512,1024]{1,0:T(8,128)(2,1)} %get-tuple-element.8) | data formatting | bytes 2097152
  167.0 0.0 copy-done
  167.0 0.6 copy.14
Async XLA Ops:
  164.8 2.3 %copy-start = (f32[1,512]{1,0:T(1,128)S(1)}, f32[1,512]{1,0:T(1,128)}, u32[]{:S(2)}) copy-start(f32[1,512]{1,0:T(1,128)} %get-tuple-element.5) | copy-start | bytes 6148

commit v4 on v3

--- a/solution.py
+++ b/solution.py
@@ -182,6 +182,12 @@
         weights.own(p)
     hg[tp] = hid[...]
 
+    my_rows = pl.ds(pl.multiple_of(spot * 64, 64), 64)
+    for k in range(1, 8):
+        slot = lax.rem(spot + k, 8)
+        rows = pl.ds(pl.multiple_of(slot * 64, 64), 64)
+        send(wo.at[rows], dealt.at[spot], r_send.at[k], r_recv.at[k], (slot * 2 + core, tp))
+    dealt[spot] = wo[my_rows]
     own = assignment[pl.ds(pl.multiple_of(zero * ROWS, ROWS), ROWS)].reshape(1, ROWS)
     row_id = lax.broadcasted_iota(jnp.int32, (ROWS, ROWS), 0)
     col_id = lax.broadcasted_iota(jnp.int32, (ROWS, ROWS), 1)
@@ -228,14 +234,14 @@
         weights.line(1, p)
         weights.opposite(0, p)
 
-    my_rows = pl.ds(pl.multiple_of(spot * 64, 64), 64)
-    for k in range(1, 8):
-        slot = lax.rem(spot + k, 8)
-        rows = pl.ds(pl.multiple_of(slot * 64, 64), 64)
-        send(wo.at[rows], dealt.at[spot], r_send.at[k], r_recv.at[k], (slot * 2 + core, tp))
-    dealt[spot] = wo[my_rows]
     for p in range(4):
         weights.opposite(1, p)
+    for k in range(1, 8):
+        arrived(dealt.at[lax.rem(spot + 8 - k, 8)], r_recv.at[k])
+    for k in range(1, 8):
+        to = lax.rem(tp + k, 8)
+        send(dealt.at[to], wog.at[core, tp, my_rows], q_send.at[k], q_recv.at[k], (zero, to))
+    wog[core, tp, my_rows] = dealt[tp]
     copied_on(weights, range(4))
 
     def project(index):
@@ -250,12 +256,6 @@
     project(tp)
     project(tp_of(0, 1))
     project(tp_of(0, -1))
-    for k in range(1, 8):
-        arrived(dealt.at[lax.rem(spot + 8 - k, 8)], r_recv.at[k])
-    for k in range(1, 8):
-        to = lax.rem(tp + k, 8)
-        send(dealt.at[to], wog.at[core, tp, my_rows], q_send.at[k], q_recv.at[k], (zero, to))
-    wog[core, tp, my_rows] = dealt[tp]
     project(tp_of(0, 2))
     project(tp_of(1, 0))
     for p in range(4):

time: 169 us -> 167 us (0.988)
  Pallas kernels: 164 us -> 161 us
    pallas_call x1, Pallas kernels: 164 us -> 161 us  [shards(): pl.pallas_call(layer, out_shape=(jax.ShapeDtypeStruct((ROWS, FEATURES), B...]
where the time goes in v4:
time: 167 us; the launch traced here: 165 us
  Pallas kernels  161 us (96%)
  local copies, waits for them, and re-layouts  2.85 us (2%)
    pallas_call x1, Pallas kernels, shards(): pl.pallas_call(layer, out_shape=(jax.ShapeDtypeStruct((ROWS, FEATURES), B...  161 us

profile of v4, /device:TPU:1, one launch (start us, length us, event | category | flops | bytes accessed | tf_op | source)
XLA Modules:
  0.0 165.0 jit_solution(11495607395957914703)
XLA Ops:
  0.6 161.5 %layer.1 = (bf16[512,1024]{1,0:T(8,128)(2,1)}, f32[1,512]{1,0:T(1,128)}) custom-call(bf16[512,1024]{1,0:T(8,128)(2,1)} %hid.1, s32[8192]{0:T(1024)} %assignment.1, bf16[8192]{0:T(1024)(128)(2,1)} %gain.1, bf16[8192]{0:T(1024)(128)(2,1)} %head.1, bf16[512,512]{1,0:T(8,128)(2,1)} %wq.1, bf16[512,128]{1,0:T(8,128)(2,1)} %wk.1, bf16[512,128]{1,0:T(8,128)(2,1)} %wv.1, ...), custom_call_target="tpu_custom_call" | custom-call | tf_op jit(solution)/shard_map/layer/pallas_call | solution.py:429
  162.1 0.0 copy-start
  162.1 2.3 %copy.13 = bf16[512,1024]{1,0:T(8,128)(2,1)} copy(bf16[512,1024]{1,0:T(8,128)(2,1)} %get-tuple-element.8) | data formatting | bytes 2097152
  164.4 0.0 copy-done
  164.4 0.6 copy.14
Async XLA Ops:
  162.1 2.3 %copy-start = (f32[1,512]{1,0:T(1,128)S(1)}, f32[1,512]{1,0:T(1,128)}, u32[]{:S(2)}) copy-start(f32[1,512]{1,0:T(1,128)} %get-tuple-element.5) | copy-start | bytes 6148

commit v5 on v4

--- a/solution.py
+++ b/solution.py
@@ -171,7 +171,7 @@
             lax.rem(index, 2), pl.ds(p // 2 * 4, 4), pl.ds(pl.multiple_of(lax.div(index, 2) * 64, 64), 64),
             pl.ds(0 if p in (0, 3) else 256, 256),
         ],
-        lambda far, dz: spot_of(far, dz) * 2 + core, zero_dev, 4, o_send, o_recv, False, True,
+        lambda far, dz: spot_of(far, dz) * 2 + core, zero_dev, 4, o_send, o_recv, True, True, 1,
     )
     a_rows = ROWS // A_PIECES
     attended = Gather(
@@ -350,6 +350,8 @@
     output(0, tp_of(0, -1))
     output(0, tp_of(0, 2))
     output(0, tp_of(1, 0))
+    for step in range(2, 4):
+        w_out.opposite(0, step)
     for p in range(A_ENDS, 4):
         attended.line(1, p)
     output(0, tp_of(1, 1))
@@ -362,7 +364,6 @@
     w_out.line(0, 2)
     w_out.line(1, 2)
     for step in range(2, 4):
-        w_out.opposite(0, step)
         w_out.opposite(1, step)
     copied_on(w_out, (1, 2))
     for far, d in ((0, 0), (0, 1), (0, -1), (0, 2), (1, 0), (1, 1), (1, -1), (1, 2)):

time: 167 us -> 170 us (1.018)
  Pallas kernels: 161 us -> 164 us
    pallas_call x1, Pallas kernels: 161 us -> 164 us  [shards(): pl.pallas_call(layer, out_shape=(jax.ShapeDtypeStruct((ROWS, FEATURES), B...]
where the time goes in v5:
time: 170 us; the launch traced here: 168 us
  Pallas kernels  164 us (96%)
  local copies, waits for them, and re-layouts  2.85 us (2%)
    pallas_call x1, Pallas kernels, shards(): pl.pallas_call(layer, out_shape=(jax.ShapeDtypeStruct((ROWS, FEATURES), B...  164 us

profile of v5, /device:TPU:1, one launch (start us, length us, event | category | flops | bytes accessed | tf_op | source)
XLA Modules:
  0.0 167.9 jit_solution(14745473563313725779)
XLA Ops:
  0.6 164.4 %layer.1 = (bf16[512,1024]{1,0:T(8,128)(2,1)}, f32[1,512]{1,0:T(1,128)}) custom-call(bf16[512,1024]{1,0:T(8,128)(2,1)} %hid.1, s32[8192]{0:T(1024)} %assignment.1, bf16[8192]{0:T(1024)(128)(2,1)} %gain.1, bf16[8192]{0:T(1024)(128)(2,1)} %head.1, bf16[512,512]{1,0:T(8,128)(2,1)} %wq.1, bf16[512,128]{1,0:T(8,128)(2,1)} %wk.1, bf16[512,128]{1,0:T(8,128)(2,1)} %wv.1, ...), custom_call_target="tpu_custom_call" | custom-call | tf_op jit(solution)/shard_map/layer/pallas_call | solution.py:430
  165.1 0.0 copy-start
  165.1 2.3 %copy.13 = bf16[512,1024]{1,0:T(8,128)(2,1)} copy(bf16[512,1024]{1,0:T(8,128)(2,1)} %get-tuple-element.8) | data formatting | bytes 2097152
  167.3 0.0 copy-done
  167.3 0.6 copy.14
Async XLA Ops:
  165.1 2.3 %copy-start = (f32[1,512]{1,0:T(1,128)S(1)}, f32[1,512]{1,0:T(1,128)}, u32[]{:S(2)}) copy-start(f32[1,512]{1,0:T(1,128)} %get-tuple-element.5) | copy-start | bytes 6148
